TPU v7x, 256 devices: a whole 4x4x8 slice. The times are simulated.
256 devices in a mesh: dp: 16 (over x, z_lo), expert: 16 (over z_hi, y, core).
Axes of the slice: x: 4, y: 4, z: 8 (z_hi: 2, z_lo: 4; z = z_hi * 4 + z_lo), core: 2. Of those that a mesh axis runs over, the one named last changes fastest.
Arguments:
- tokens: bfloat16 [8192, 4096], P('expert', 'dp'), may hold values from -6 to 6
- expert_ids: int32 [8192, 2], P('expert'), may hold values from 0 to 31, all different within a row; in each aligned block of 512 rows (0 to 511, 512 to 1023, ...) at most 64 rows name the same one
- gate_values: float32 [8192, 2], P('expert'), may hold values from 0.2 to 1
- w_in: bfloat16 [32, 4096, 1536], P('expert', 'dp'), may hold values from -0.09375 to 0.09375
- w_out: bfloat16 [32, 1536, 4096], P('expert', None, 'dp'), may hold values from -0.15625 to 0.15625
- grad_out: bfloat16 [8192, 4096], P('expert', 'dp'), may hold values from -3 to 3
Outputs:
- mixed: bfloat16 [8192, 4096], P('expert', 'dp')
- grad_tokens: bfloat16 [8192, 4096], P('expert', 'dp')
- grad_w_in: float32 [32, 4096, 1536], P('expert', 'dp')
- grad_w_out: float32 [32, 1536, 4096], P('expert', None, 'dp')
Inputs may be any that keep to these rules, and one draw needn't show every extreme that they name: `expert_ids`: each row names 2 different experts; among the 512 rows of one index of expert no expert is named by more than 64 rows, a bound that some block reaches.
All inputs are finite; a program needn't handle non-finite values.
Results may differ from a plain program's by a relative error of at most 0.03.
Values may be sent and summed in bfloat16 or wider, within the bound.
A program may use at most 128 MiB of HBM per device.

v0:
```python
import jax
import jax.numpy as jnp
from jax import lax
from jax.sharding import PartitionSpec as P

TOP = 2
EXP_DEV = 2


def gelu_value(pre):
    return jax.nn.gelu(pre, approximate=True)


def gelu_slope(pre):
    value, pullback = jax.vjp(gelu_value, pre)
    return pullback(jnp.ones_like(pre))[0]


def slot_index(expert_ids, num_experts, capacity):
    flat = expert_ids.reshape(-1)
    onehot = (flat[:, None] == jnp.arange(num_experts, dtype=jnp.int32)[None, :]).astype(jnp.int32)
    before = jnp.cumsum(onehot, axis=0) - onehot
    position = jnp.sum(before * onehot, axis=1)
    return flat * capacity + position


def sum_apart(partial_value):
    return lax.psum_scatter(
        partial_value.astype(jnp.bfloat16), "dp", scatter_dimension=0, tiled=True
    ).astype(jnp.float32)


def gather_apart(share):
    return lax.all_gather(share, "dp", axis=0, tiled=True)


def send_back(slot_rows):
    return lax.all_to_all(slot_rows, "expert", split_axis=0, concat_axis=0, tiled=True)


def body(tokens, expert_ids, gate_values, w_in, w_out, grad_out):
    groups = lax.axis_size("expert")
    tok_rows = tokens.shape[0]
    width = tokens.shape[1]
    hidden = w_in.shape[2]
    num_experts = EXP_DEV * groups
    capacity = 2 * tok_rows * TOP // num_experts
    total = num_experts * capacity
    slots = slot_index(expert_ids, num_experts, capacity)
    pair_rows = jnp.repeat(tokens, TOP, axis=0)
    scaled = (
        (gate_values[:, :, None] * grad_out[:, None, :].astype(jnp.float32))
        .astype(jnp.bfloat16)
        .reshape(tok_rows * TOP, width)
    )
    send_rows = (
        jnp.zeros((total, width), jnp.bfloat16)
        .at[slots]
        .set(pair_rows)
        .reshape(groups, EXP_DEV * capacity, width)
    )
    send_grads = (
        jnp.zeros((total, width), jnp.bfloat16)
        .at[slots]
        .set(scaled)
        .reshape(groups, EXP_DEV * capacity, width)
    )

    def inbound(rows):
        return rows.reshape(groups, EXP_DEV, capacity, width)

    got_rows = inbound(lax.all_to_all(send_rows, "expert", split_axis=0, concat_axis=0, tiled=True))
    pre_share = sum_apart(
        jnp.einsum("slcd,ldh->slch", got_rows, w_in, preferred_element_type=jnp.float32).reshape(
            -1, hidden
        )
    )
    act = gather_apart(gelu_value(pre_share).astype(jnp.bfloat16)).reshape(
        groups, EXP_DEV, capacity, hidden
    )
    result = jnp.einsum("slch,lhd->slcd", act, w_out, preferred_element_type=jnp.float32).astype(
        jnp.bfloat16
    )
    arrived = send_back(result.reshape(groups, EXP_DEV * capacity, width)).reshape(total, width)
    picked = arrived[slots].reshape(tok_rows, TOP, width).astype(jnp.float32)
    mixed = jnp.sum(gate_values[:, :, None] * picked, axis=1).astype(jnp.bfloat16)
    got_grads = inbound(
        lax.all_to_all(send_grads, "expert", split_axis=0, concat_axis=0, tiled=True)
    )
    slope_share = sum_apart(
        jnp.einsum("slcd,lhd->slch", got_grads, w_out, preferred_element_type=jnp.float32).reshape(
            -1, hidden
        )
    )
    delta = gather_apart((slope_share * gelu_slope(pre_share)).astype(jnp.bfloat16)).reshape(
        groups, EXP_DEV, capacity, hidden
    )
    grad_w_out = jnp.einsum("slch,slcd->lhd", act, got_grads, preferred_element_type=jnp.float32)
    grad_w_in = jnp.einsum("slcd,slch->ldh", got_rows, delta, preferred_element_type=jnp.float32)
    back = jnp.einsum("slch,ldh->slcd", delta, w_in, preferred_element_type=jnp.float32).astype(
        jnp.bfloat16
    )
    returned = send_back(back.reshape(groups, EXP_DEV * capacity, width)).reshape(total, width)
    gathered = returned[slots].reshape(tok_rows, TOP, width).astype(jnp.float32)
    grad_tokens = jnp.sum(gathered, axis=1).astype(jnp.bfloat16)
    return (mixed, grad_tokens, grad_w_in, grad_w_out)


def solution(mesh):
    return jax.shard_map(
        body,
        mesh=mesh,
        in_specs=(
            P("expert", "dp"),
            P("expert", None),
            P("expert", None),
            P("expert", "dp", None),
            P("expert", None, "dp"),
            P("expert", "dp"),
        ),
        out_specs=(
            P("expert", "dp"),
            P("expert", "dp"),
            P("expert", "dp", None),
            P("expert", None, "dp"),
        ),
        check_vma=False,
    )
```

profile of v0, /device:TPU:1, one launch (start us, length us, event | category | flops | bytes accessed | tf_op | source)
XLA Modules:
  0.0 750.2 jit_solution(10159270436512219492)
XLA Ops:
  7.2 0.0 copy-start
  7.2 0.0 reduce-scatter.5.cloned.1.call-start
  7.2 0.9 copy.13
  8.2 0.2 eq.29
  8.3 0.2 eq.25
  8.5 0.7 broadcast_multiply_fusion
  9.2 9.0 %reduce-window.6 = s32[32,8,128]{2,1,0:T(8,128)S(1)} reduce-window(s32[32,8,128]{2,1,0:T(8,128)S(1)} %fusion.48, s32[]{:T(128)} %constant.6.clone.1), window={size=1x1x128 pad=0_0x0_0x127_0}, to_apply=%region_0.0 | reduce-window | flops 4161536 | bytes 262148 | tf_op jit(solution)/shard_map/reduce-window
  18.2 0.1 slice.12
  18.3 0.1 copy.15
  18.5 0.1 copy.16
  18.6 0.1 broadcast_add_fusion
  18.7 0.1 copy.12
  18.8 0.2 mul.92
  19.0 0.8 copy.11
  19.9 0.2 mul.99
  20.0 2.2 mul.101
  22.2 1.9 mul.102
  24.2 6.5 scatter_custom_fusion.1
  30.7 34.4 %all_to_all.20 = bf16[16,128,256]{2,1,0:T(8,128)(2,1)S(1)} all-to-all(bf16[16,128,256]{2,1,0:T(8,128)(2,1)} %bitcast.77), channel_id=1, replica_groups=mesh['dp'=16,'expert'=16] {'expert'}, dimensions={0} | all-to-all | bytes 2097152 | tf_op jit(solution)/shard_map/all_to_all | solution.py:88
  65.1 0.0 copy-start.2
  65.1 0.0 copy-done
  65.1 1.8 convert_bitcast_fusion
  66.9 3.3 copy.23
  70.3 0.0 copy-done.2
  70.3 0.0 reduce-scatter.5.cloned.1.call-update
  70.3 0.0 reduce-scatter.3.cloned.1.call-start
  70.4 0.9 copy-done.6
  71.2 0.3 broadcast_in_dim.2
  71.5 0.2 reshape.137
  71.7 5.3 scatter_custom_fusion
  77.0 45.9 %all_to_all.21 = bf16[16,128,256]{2,1,0:T(8,128)(2,1)S(1)} all-to-all(bf16[16,128,256]{2,1,0:T(8,128)(2,1)S(1)} %bitcast.79), channel_id=1, replica_groups=mesh['dp'=16,'expert'=16] {'expert'}, dimensions={0} | all-to-all | bytes 2097152 | tf_op jit(solution)/shard_map/all_to_all | solution.py:72
  122.9 3.6 convert_bitcast_fusion.1
  126.5 3.3 copy.18
  129.8 0.0 copy-done.4
  129.8 0.0 reduce-scatter.3.cloned.1.call-update
  129.9 0.0 all-gather.3.cloned.1.call-start
  129.9 113.1 %reduce-scatter.5.cloned.1.call-done = bf16[128,1536]{1,0:T(8,128)(2,1)} async-done(((bf16[2048,1536]{1,0:T(8,128)(2,1)}), bf16[128,1536]{1,0:T(8,128)(2,1)}) %reduce-scatter.5.cloned.1.call-update) | async-done | bytes 393232 | tf_op jit(solution)/shard_map/reduce_scatter | solution.py:28
  243.0 141.9 %reduce-scatter.3.cloned.1.call-done = bf16[128,1536]{1,0:T(8,128)(2,1)} async-done(((bf16[2048,1536]{1,0:T(8,128)(2,1)}), bf16[128,1536]{1,0:T(8,128)(2,1)}) %reduce-scatter.3.cloned.1.call-update) | async-done | bytes 393232 | tf_op jit(solution)/shard_map/reduce_scatter | solution.py:28
  385.0 2.6 fusion.34
  387.5 0.0 all-gather.3.cloned.1.call-update
  387.5 0.0 all-gather.5.cloned.1.call-start
  387.6 0.5 all-gather.5.cloned.1.call-update
  388.1 140.9 %all-gather.3.cloned.1.call-done = bf16[2048,1536]{1,0:T(8,128)(2,1)} async-done(((bf16[128,1536]{1,0:T(8,128)(2,1)}), bf16[2048,1536]{1,0:T(8,128)(2,1)}) %all-gather.3.cloned.1.call-update) | async-done | bytes 6291472 | tf_op jit(solution)/shard_map/all_gather | solution.py:34
  529.0 4.6 fusion.23
  533.6 1.0 copy.20
  534.6 7.7 %all-to-all-start.1 = ((bf16[16,128,256]{2,1,0:T(8,128)(2,1)}), bf16[16,128,256]{2,1,0:T(8,128)(2,1)S(1)}, u32[]{:S(2)}, u32[]{:S(2)}) async-start(bf16[16,128,256]{2,1,0:T(8,128)(2,1)} %bitcast.14), calls=%async_computation.2 | async-start | bytes 2097152 | tf_op jit(solution)/shard_map/all_to_all | solution.py:38
  542.3 152.2 %all-gather.5.cloned.1.call-done = bf16[2048,1536]{1,0:T(8,128)(2,1)} async-done(((bf16[128,1536]{1,0:T(8,128)(2,1)}), bf16[2048,1536]{1,0:T(8,128)(2,1)}) %all-gather.5.cloned.1.call-update) | async-done | bytes 6291472 | tf_op jit(solution)/shard_map/all_gather | solution.py:34
  694.5 5.1 fusion.18
  699.6 1.1 copy.25
  700.7 0.0 all-to-all-done.1
  700.7 7.7 %all-to-all-start.3 = ((bf16[16,128,256]{2,1,0:T(8,128)(2,1)}), bf16[16,128,256]{2,1,0:T(8,128)(2,1)}, u32[]{:S(2)}, u32[]{:S(2)}) async-start(bf16[16,128,256]{2,1,0:T(8,128)(2,1)} %bitcast.78), calls=%async_computation.5 | async-start | bytes 2097152 | tf_op jit(solution)/shard_map/all_to_all | solution.py:38
  708.4 0.0 copy-done.3
  708.4 0.0 copy-start.5
  708.4 7.1 convolution_bitcast_fusion
  715.5 0.0 copy-done.5
  715.5 6.3 convolution_bitcast_fusion.1
  721.8 3.9 gather_fusion
  725.7 0.5 reshape.116
  726.2 3.6 multiply_reduce_fusion
  729.8 6.7 all-to-all-done.3
  736.5 4.8 gather_fusion.1
  741.4 0.2 reshape.115
  741.6 2.1 reduce_sum.35
  743.6 0.0 copy-done.1
  (10 shorter events, 0.1 us)
Async XLA Ops:
  7.2 57.9 %copy-start = (bf16[2,1536,256]{2,1,0:T(8,128)(2,1)S(1)}, bf16[2,1536,256]{2,1,0:T(8,128)(2,1)}, u32[]{:S(2)}) copy-start(bf16[2,1536,256]{2,1,0:T(8,128)(2,1)} %param.10) | copy-start | bytes 4718596
  7.2 235.9 %reduce-scatter.5.cloned.1.call-start = ((), (), s32[]{:S(2)}) async-start(), calls=%async_computation.8 | async-start | bytes 6684672 | tf_op jit(solution)/shard_map/reduce_scatter | solution.py:28
  65.1 5.2 copy-start.2
  70.3 1.0 copy-start.6
  70.3 314.7 %reduce-scatter.3.cloned.1.call-start = ((), (), s32[]{:S(2)}) async-start(), calls=%async_computation.6 | async-start | bytes 6684672 | tf_op jit(solution)/shard_map/reduce_scatter | solution.py:28
  122.9 6.9 copy-start.4
  129.9 399.1 %all-gather.3.cloned.1.call-start = ((), (), s32[]{:S(2)}) async-start(), calls=%async_computation.7 | async-start | bytes 6684672 | tf_op jit(solution)/shard_map/all_gather | solution.py:34
  387.5 306.9 %all-gather.5.cloned.1.call-start = ((), (), s32[]{:S(2)}) async-start(), calls=%async_computation.9 | async-start | bytes 6684672 | tf_op jit(solution)/shard_map/all_gather | solution.py:34
  534.6 166.1 %all-to-all-start.1 = ((bf16[16,128,256]{2,1,0:T(8,128)(2,1)}), bf16[16,128,256]{2,1,0:T(8,128)(2,1)S(1)}, u32[]{:S(2)}, u32[]{:S(2)}) async-start(bf16[16,128,256]{2,1,0:T(8,128)(2,1)} %bitcast.14), calls=%async_computation.2 | async-start | bytes 2097152 | tf_op jit(solution)/shard_map/all_to_all | solution.py:38
  694.5 13.9 %copy-start.3 = (bf16[16,128,256]{2,1,0:T(8,128)(2,1)S(1)}, bf16[16,128,256]{2,1,0:T(8,128)(2,1)}, u32[]{:S(2)}) copy-start(bf16[16,128,256]{2,1,0:T(8,128)(2,1)} %copy-done.2) | copy-start | bytes 3145732
  700.7 35.8 %all-to-all-start.3 = ((bf16[16,128,256]{2,1,0:T(8,128)(2,1)}), bf16[16,128,256]{2,1,0:T(8,128)(2,1)}, u32[]{:S(2)}, u32[]{:S(2)}) async-start(bf16[16,128,256]{2,1,0:T(8,128)(2,1)} %bitcast.78), calls=%async_computation.5 | async-start | bytes 2097152 | tf_op jit(solution)/shard_map/all_to_all | solution.py:38
  708.4 7.1 copy-start.5
  721.8 21.9 %copy-start.1 = (bf16[2,1536,256]{2,1,0:T(8,128)(2,1)S(1)}, bf16[2,1536,256]{2,1,0:T(8,128)(2,1)}, u32[]{:S(2)}) copy-start(bf16[2,1536,256]{2,1,0:T(8,128)(2,1)} %param.10) | copy-start | bytes 4718596
Sparse Core Ops, SparseCore 0:
  70.4 172.5 reduce-scatter.4
  245.6 139.3 reduce-scatter.2
  387.7 141.2 all-gather.2
  530.6 163.7 all-gather.4
where the time goes:
time: 751 us; the launch traced here: 750 us
  waiting for transfers between devices  555 us (74%)
  blocking collectives  80.3 us (11%)
  local copies, waits for them, and re-layouts  32 us (4%)
  matrix products  28.5 us (4%)
  other arithmetic  24.6 us (3%)
  starting transfers between devices  15.5 us (2%)
  between operations  14 us (2%)
    all_gather x2, waiting for transfers between devices, gather_apart(): return lax.all_gather(share, 'dp', axis=0, tiled=True)  293 us
    reduce_scatter x2, waiting for transfers between devices, sum_apart(): lax.psum_scatter(partial_value.astype(jnp.bfloat16), 'dp', scatter_dimens...  255 us
    all_to_all x1, blocking collectives, body(): lax.all_to_all(send_rows, 'expert', split_axis=0, concat_axis=0, tiled=True)  45.9 us
    all_to_all x1, blocking collectives, body(): lax.all_to_all(send_grads, 'expert', split_axis=0, concat_axis=0, tiled=T...  34.4 us
    all_to_all x2, starting transfers between devices, send_back(): lax.all_to_all(slot_rows, 'expert', split_axis=0, concat_axis=0, tiled=True)  15.3 us
  transfers between devices with their start and end apart: 6, of which 5 were waited for; matrix products, arithmetic and copies ran while one was open for 6% of the time, Pallas kernels for 0%

commit v1 on v0

--- a/solution.py
+++ b/solution.py
@@ -31,7 +31,9 @@
 
 
 def gather_apart(share):
-    return lax.all_gather(share, "dp", axis=0, tiled=True)
+    return jnp.concatenate(
+        lax.all_to_all(jnp.stack([share] * lax.axis_size("dp")), "dp", 0, 0), axis=0
+    )
 
 
 def send_back(slot_rows):

time: 751 us -> 763 us (1.016)
  waiting for transfers between devices: 555 us -> 411 us
  blocking collectives: 80.3 us -> 223 us
    all_gather x2 -> x0, waiting for transfers between devices: 293 us -> none  [gather_apart(): return lax.all_gather(share, 'dp', axis=0, tiled=True)]
    all_to_all x0 -> x1, blocking collectives: none -> 143 us  [gather_apart(): lax.all_to_all(jnp.stack([share] * lax.axis_size('dp')), 'dp', 0, 0)]
    all_to_all x0 -> x1, waiting for transfers between devices: none -> 135 us  [gather_apart(): lax.all_to_all(jnp.stack([share] * lax.axis_size('dp')), 'dp', 0, 0)]
    all_to_all x2, waiting for transfers between devices: 6.72 us -> 21.3 us  [send_back(): lax.all_to_all(slot_rows, 'expert', split_axis=0, concat_axis=0, tiled=True)]
  transfers between devices with their start and end apart: 6 -> 5, of which waited for: 5 -> 4; matrix products, arithmetic and copies ran while one was open for 6% -> 6% of each run, Pallas kernels for 0% -> 0%
where the time goes in v1:
time: 763 us; the launch traced here: 760 us
  waiting for transfers between devices  411 us (54%)
  blocking collectives  223 us (29%)
  local copies, waits for them, and re-layouts  37.7 us (5%)
  matrix products  28.3 us (4%)
  other arithmetic  23.7 us (3%)
  starting transfers between devices  22.5 us (3%)
  between operations  14.2 us (2%)
    reduce_scatter x2, waiting for transfers between devices, sum_apart(): lax.psum_scatter(partial_value.astype(jnp.bfloat16), 'dp', scatter_dimens...  254 us
    all_to_all x1, blocking collectives, gather_apart(): lax.all_to_all(jnp.stack([share] * lax.axis_size('dp')), 'dp', 0, 0)  143 us
    all_to_all x1, waiting for transfers between devices, gather_apart(): lax.all_to_all(jnp.stack([share] * lax.axis_size('dp')), 'dp', 0, 0)  135 us
    all_to_all x1, blocking collectives, body(): lax.all_to_all(send_rows, 'expert', split_axis=0, concat_axis=0, tiled=True)  45.9 us
    all_to_all x1, blocking collectives, body(): lax.all_to_all(send_grads, 'expert', split_axis=0, concat_axis=0, tiled=T...  34.4 us
    all_to_all x2, waiting for transfers between devices, send_back(): lax.all_to_all(slot_rows, 'expert', split_axis=0, concat_axis=0, tiled=True)  21.3 us
    all_to_all x2, starting transfers between devices, send_back(): lax.all_to_all(slot_rows, 'expert', split_axis=0, concat_axis=0, tiled=True)  17.7 us
  transfers between devices with their start and end apart: 5, of which 4 were waited for; matrix products, arithmetic and copies ran while one was open for 6% of the time, Pallas kernels for 0%

profile of v1, /device:TPU:1, one launch (start us, length us, event | category | flops | bytes accessed | tf_op | source)
XLA Modules:
  0.0 760.4 jit_solution(5482359741221395750)
XLA Ops:
  7.2 0.0 copy-start
  7.2 0.0 reduce-scatter.5.cloned.1.call-start
  7.2 0.9 copy.13
  8.2 0.2 eq.29
  8.3 0.2 eq.25
  8.5 0.7 broadcast_multiply_fusion
  9.2 9.0 %reduce-window.6 = s32[32,8,128]{2,1,0:T(8,128)S(1)} reduce-window(s32[32,8,128]{2,1,0:T(8,128)S(1)} %fusion.48, s32[]{:T(128)} %constant.6.clone.1), window={size=1x1x128 pad=0_0x0_0x127_0}, to_apply=%region_0.0 | reduce-window | flops 4161536 | bytes 262148 | tf_op jit(solution)/shard_map/reduce-window
  18.2 0.1 slice.12
  18.3 0.1 copy.15
  18.5 0.1 copy.16
  18.6 0.1 broadcast_add_fusion
  18.7 0.1 copy.12
  18.8 0.2 mul.92
  19.0 0.8 copy.11
  19.9 0.2 mul.99
  20.0 2.2 mul.101
  22.2 1.9 mul.102
  24.2 6.5 scatter_custom_fusion.1
  30.7 34.4 %all_to_all.30 = bf16[16,128,256]{2,1,0:T(8,128)(2,1)S(1)} all-to-all(bf16[16,128,256]{2,1,0:T(8,128)(2,1)} %bitcast.79), channel_id=1, replica_groups=mesh['dp'=16,'expert'=16] {'expert'}, dimensions={0} | all-to-all | bytes 2097152 | tf_op jit(solution)/shard_map/all_to_all | solution.py:90
  65.1 0.0 copy-start.1
  65.1 1.0 copy-done.1
  66.1 0.0 copy-done
  66.1 1.8 convert_bitcast_fusion
  67.9 3.3 copy.23
  71.3 0.0 copy-start.4
  71.3 0.0 reduce-scatter.5.cloned.1.call-update
  71.3 0.0 reduce-scatter.3.cloned.1.call-start
  71.3 0.9 copy-done.4
  72.2 0.3 broadcast_in_dim.2
  72.5 0.2 reshape.133
  72.7 5.3 scatter_custom_fusion
  78.0 45.9 %all_to_all.31 = bf16[16,128,256]{2,1,0:T(8,128)(2,1)S(1)} all-to-all(bf16[16,128,256]{2,1,0:T(8,128)(2,1)S(1)} %bitcast.82), channel_id=1, replica_groups=mesh['dp'=16,'expert'=16] {'expert'}, dimensions={0} | all-to-all | bytes 2097152 | tf_op jit(solution)/shard_map/all_to_all | solution.py:74
  123.9 0.0 copy-start.2
  123.9 1.0 copy-done.2
  124.9 3.2 convert_bitcast_fusion.1
  128.1 3.3 copy.18
  131.4 0.0 reduce-scatter.3.cloned.1.call-update
  131.4 112.6 %reduce-scatter.5.cloned.1.call-done = bf16[128,1536]{1,0:T(8,128)(2,1)} async-done(((bf16[2048,1536]{1,0:T(8,128)(2,1)}), bf16[128,1536]{1,0:T(8,128)(2,1)}) %reduce-scatter.5.cloned.1.call-update) | async-done | bytes 393232 | tf_op jit(solution)/shard_map/reduce_scatter | solution.py:28
  244.0 141.9 %reduce-scatter.3.cloned.1.call-done = bf16[128,1536]{1,0:T(8,128)(2,1)} async-done(((bf16[2048,1536]{1,0:T(8,128)(2,1)}), bf16[128,1536]{1,0:T(8,128)(2,1)}) %reduce-scatter.3.cloned.1.call-update) | async-done | bytes 393232 | tf_op jit(solution)/shard_map/reduce_scatter | solution.py:28
  385.9 1.7 fusion.34
  387.6 0.6 stack.4
  388.3 142.7 %all_to_all.32 = bf16[16,128,1536]{2,1,0:T(8,128)(2,1)} all-to-all(bf16[16,128,1536]{2,1,0:T(8,128)(2,1)S(1)} %stack.4), channel_id=1, replica_groups=mesh['dp'=16,'expert'=16] {'dp'}, dimensions={0} | all-to-all | bytes 12582912 | tf_op jit(solution)/shard_map/all_to_all | solution.py:35
  531.0 3.2 stack.5
  534.2 4.7 all-to-all-start.4
  538.9 4.6 fusion.23
  543.4 1.0 copy.20
  544.5 135.1 %all-to-all-done.4 = bf16[16,128,1536]{2,1,0:T(8,128)(2,1)} async-done(((bf16[16,128,1536]{2,1,0:T(8,128)(2,1)}), bf16[16,128,1536]{2,1,0:T(8,128)(2,1)}, u32[]{:S(2)}, u32[]{:S(2)}) %all-to-all-start.4) | async-done | bytes 6291488 | tf_op jit(solution)/shard_map/all_to_all | solution.py:35
  679.6 10.8 %all-to-all-start.2 = ((bf16[16,128,256]{2,1,0:T(8,128)(2,1)}), bf16[16,128,256]{2,1,0:T(8,128)(2,1)S(1)}, u32[]{:S(2)}, u32[]{:S(2)}) async-start(bf16[16,128,256]{2,1,0:T(8,128)(2,1)} %bitcast.81), calls=%async_computation.3 | async-start | bytes 2097152 | tf_op jit(solution)/shard_map/all_to_all | solution.py:40
  690.4 5.0 fusion.18
  695.4 1.1 copy.25
  696.5 21.3 %all-to-all-done.2 = bf16[16,128,256]{2,1,0:T(8,128)(2,1)S(1)} async-done(((bf16[16,128,256]{2,1,0:T(8,128)(2,1)}), bf16[16,128,256]{2,1,0:T(8,128)(2,1)S(1)}, u32[]{:S(2)}, u32[]{:S(2)}) %all-to-all-start.2) | async-done | bytes 1048608 | tf_op jit(solution)/shard_map/all_to_all | solution.py:40
  717.9 6.9 all-to-all-start.5
  724.8 0.0 copy-start.3
  724.8 7.3 convolution_bitcast_fusion
  732.1 0.0 copy-done.3
  732.1 6.3 convolution_bitcast_fusion.1
  738.4 3.9 gather_fusion
  742.4 0.5 reshape.112
  742.9 3.6 multiply_reduce_fusion
  746.5 0.0 all-to-all-done.5
  746.5 4.8 gather_fusion.1
  751.3 0.2 reshape.111
  751.5 2.1 reduce_sum.35
  (6 shorter events, 0.1 us)
Async XLA Ops:
  7.2 58.9 %copy-start = (bf16[2,1536,256]{2,1,0:T(8,128)(2,1)S(1)}, bf16[2,1536,256]{2,1,0:T(8,128)(2,1)}, u32[]{:S(2)}) copy-start(bf16[2,1536,256]{2,1,0:T(8,128)(2,1)} %param.10) | copy-start | bytes 4718596
  7.2 236.8 %reduce-scatter.5.cloned.1.call-start = ((), (), s32[]{:S(2)}) async-start(), calls=%async_computation.9 | async-start | bytes 6684672 | tf_op jit(solution)/shard_map/reduce_scatter | solution.py:28
  65.1 1.0 copy-start.1
  71.3 0.9 copy-start.4
  71.3 314.7 %reduce-scatter.3.cloned.1.call-start = ((), (), s32[]{:S(2)}) async-start(), calls=%async_computation.8 | async-start | bytes 6684672 | tf_op jit(solution)/shard_map/reduce_scatter | solution.py:28
  123.9 1.0 copy-start.2
  534.2 145.4 %all-to-all-start.4 = ((bf16[16,128,1536]{2,1,0:T(8,128)(2,1)}), bf16[16,128,1536]{2,1,0:T(8,128)(2,1)}, u32[]{:S(2)}, u32[]{:S(2)}) async-start(bf16[16,128,1536]{2,1,0:T(8,128)(2,1)} %stack.5), calls=%async_computation.6 | async-start | bytes 12582912 | tf_op jit(solution)/shard_map/all_to_all | solution.py:35
  679.6 38.3 %all-to-all-start.2 = ((bf16[16,128,256]{2,1,0:T(8,128)(2,1)}), bf16[16,128,256]{2,1,0:T(8,128)(2,1)S(1)}, u32[]{:S(2)}, u32[]{:S(2)}) async-start(bf16[16,128,256]{2,1,0:T(8,128)(2,1)} %bitcast.81), calls=%async_computation.3 | async-start | bytes 2097152 | tf_op jit(solution)/shard_map/all_to_all | solution.py:40
  717.9 28.6 %all-to-all-start.5 = ((bf16[16,128,256]{2,1,0:T(8,128)(2,1)}), bf16[16,128,256]{2,1,0:T(8,128)(2,1)}, u32[]{:S(2)}, u32[]{:S(2)}) async-start(bf16[16,128,256]{2,1,0:T(8,128)(2,1)} %bitcast.80), calls=%async_computation.7 | async-start | bytes 2097152 | tf_op jit(solution)/shard_map/all_to_all | solution.py:40
  724.8 7.4 copy-start.3
Sparse Core Ops, SparseCore 0:
  71.4 172.5 reduce-scatter.4
  246.6 139.3 reduce-scatter.2
